TPU v7x, 128 devices: a whole 4x4x4 slice. The times are simulated.
128 devices in a mesh: zg: 4 (over z_hi, core), xy: 32 (over z_lo, y, x).
Axes of the slice: x: 4, y: 4, z: 4 (z_hi: 2, z_lo: 2; z = z_hi * 2 + z_lo), core: 2. Of those that a mesh axis runs over, the one named last changes fastest.
Arguments:
- dipole_field: bfloat16 [2, 3, 16, 512, 256], P(None, None, 'zg', 'xy'), may hold values from -6 to 6
- material: int32 [16, 512, 2], P('zg', 'xy'), may hold values from 0 to 3
- alpha_table: float32 [4, 2, 3, 3], replicated, may hold values from -3 to 3
- green_spectrum: bfloat16 [2, 6, 32, 1024, 512], P(None, None, 'xy', None, 'zg'), may hold values from -6 to 6
- green_scale: float32 [6, 32], P(None, 'xy'), may hold values from 0.5 to 2
Outputs:
- scattered_field: bfloat16 [2, 3, 16, 512, 256], P(None, None, 'zg', 'xy')
All inputs are finite; a program needn't handle non-finite values.
Results may differ from a plain program's by a relative error of at most 0.019.
Values may be sent and summed in bfloat16 or wider, within the bound.
A program may use at most 128 MiB of HBM per device.

v0:
```python
import functools
import math

import jax
import jax.numpy as jnp
import ml_dtypes
import numpy as np
from jax import lax
from jax.experimental import pallas as pl
from jax.experimental.pallas import tpu as pltpu
from jax.sharding import PartitionSpec as P

MESH = pl.DeviceIdType.MESH
F32 = jnp.float32
BF16 = jnp.bfloat16

pairing = ((0, 3, 4), (3, 1, 5), (4, 5, 2))


def dft_table(count_in, count_out, length, direction):
    phases = (np.arange(count_in)[:, None] * np.arange(count_out)[None, :] % length).astype(np.float32)
    phases = phases * np.float32(2.0 * math.pi / length)
    cosine = np.cos(phases).astype(ml_dtypes.bfloat16).astype(np.float32)
    sine = (np.float32(direction) * np.sin(phases)).astype(ml_dtypes.bfloat16).astype(np.float32)
    return cosine, sine


def tables_of(rows_y, planes_z, rows_x, n_zg, n_xy):
    length_y, length_z, length_x = 2 * rows_y, 2 * planes_z, 2 * rows_x
    block_y = length_y // n_zg
    local_x = rows_x // n_xy
    eye = np.eye(local_x, dtype=np.float32)
    c, s = dft_table(rows_y, length_y, length_y, -1.0)
    full = np.block([[c, s], [-s, c]]).reshape(2 * rows_y, 2, n_zg, block_y)
    forward_y = full.transpose(0, 2, 1, 3).reshape(2 * rows_y, 2 * length_y)
    c, s = dft_table(planes_z, length_z, length_z, -1.0)
    forward_z = np.concatenate([np.kron(c.T, eye), np.kron(s.T, eye)], axis=1)
    c, s = dft_table(rows_x, length_x, length_x, -1.0)
    forward_x = np.concatenate([c.T, s.T], axis=1)
    c, s = dft_table(length_x, rows_x, length_x, 1.0)
    inverse_x = np.concatenate([c.T, s.T], axis=1)
    c, s = dft_table(length_z, planes_z, length_z, 1.0)
    inverse_z = np.concatenate([np.kron(c.T, eye), np.kron(s.T, eye)], axis=1)
    c, s = dft_table(length_y, rows_y, length_y, 1.0)
    full = np.block([[c, s], [-s, c]]).reshape(2, n_zg, block_y, 2 * rows_y)
    inverse_y = full.transpose(1, 0, 2, 3).reshape(2 * length_y, 2 * rows_y)
    return [
        np.ascontiguousarray(t).astype(ml_dtypes.bfloat16)
        for t in (forward_y, forward_z, forward_x, inverse_x, inverse_z, inverse_y)
    ]


def times_i(pair):
    half = pair.shape[1] // 2
    return jnp.concatenate([-pair[:, half:], pair[:, :half]], axis=1)


def stacked(pair):
    return jnp.concatenate([pair, times_i(pair)], axis=0)


def dot(a, b):
    return jnp.dot(a, b, preferred_element_type=F32)


def kernel(
    n_zg, n_xy, norm,
    field_hbm, material_ref, alpha_ref, green_hbm, scale_ref,
    ty_hbm, tz_hbm, tx_hbm, ux_hbm, uz_hbm, uy_hbm,
    out_ref,
    field, green, ty, tz, tx, ux, uz, uy,
    mom, a_send, a_recv, b_send, b_recv, spec, prod, c_send, c_recv, d_send, d_recv,
    load_sem, a_ss, a_rs, b_ss, b_rs, c_ss, c_rs, d_ss, d_rs,
):
    g = lax.axis_index("zg")
    q = lax.axis_index("xy")
    loads = [
        pltpu.make_async_copy(src, dst, load_sem.at[index])
        for index, (src, dst) in enumerate(
            (
                (field_hbm, field), (ty_hbm, ty), (tz_hbm, tz), (tx_hbm, tx),
                (green_hbm, green), (ux_hbm, ux), (uz_hbm, uz), (uy_hbm, uy),
            )
        )
    ]
    for load in loads:
        load.start()

    barrier = pltpu.get_barrier_semaphore()

    def greet_xy(step, carry):
        peer = lax.rem(q + step, n_xy)
        pl.semaphore_signal(barrier, inc=1, device_id=(g, peer), device_id_type=MESH)
        return carry

    def greet_zg(step, carry):
        peer = lax.rem(g + step, n_zg)
        pl.semaphore_signal(barrier, inc=1, device_id=(peer, q), device_id_type=MESH)
        return carry

    lax.fori_loop(1, n_xy, greet_xy, 0)
    lax.fori_loop(1, n_zg, greet_zg, 0)

    loads[0].wait()
    planes, rows, width = field.shape[2:]
    half = width // 2
    for z in range(planes):
        for b in range(2):
            lanes = slice(b * half, (b + 1) * half)
            which = jnp.broadcast_to(material_ref[z][:, b : b + 1], (rows, half))
            masks = [which == m for m in range(3)]

            def tensor(r, i, j):
                value = jnp.full((rows, half), alpha_ref[3, r, i, j], F32)
                for m in range(3):
                    value = jnp.where(masks[m], alpha_ref[m, r, i, j], value)
                return value

            values = [[field[r, j, z, :, lanes].astype(F32) for j in range(3)] for r in range(2)]
            for i in range(3):
                real = jnp.zeros((rows, half), F32)
                imag = jnp.zeros((rows, half), F32)
                for j in range(3):
                    t_re, t_im = tensor(0, i, j), tensor(1, i, j)
                    real = real + t_re * values[0][j] - t_im * values[1][j]
                    imag = imag + t_re * values[1][j] + t_im * values[0][j]
                start = (i * planes + z) * rows
                mom[start : start + rows, b * half : (b + 1) * half] = real.astype(BF16)
                mom[start : start + rows, width + b * half : width + (b + 1) * half] = imag.astype(BF16)

    def exchange(send, recv, ss, rs, index, axis):
        count, me = (n_zg, g) if axis == "zg" else (n_xy, q)

        def step_of(step, carry):
            peer = lax.rem(me + step, count)
            target = (peer, q) if axis == "zg" else (g, peer)
            pltpu.make_async_remote_copy(
                send.at[index, peer], recv.at[index, me], ss.at[index], rs.at[index],
                device_id=target, device_id_type=MESH,
            ).start()
            return carry

        lax.fori_loop(1, count, step_of, 0)
        recv[index, me] = send[index, me]

    def arrived(recv, rs, index):
        others = recv.at[index, pl.ds(0, recv.shape[1] - 1)]
        pltpu.make_async_copy(others, others, rs.at[index]).wait()

    loads[1].wait()
    spectrum = dot(mom[...], ty[...]).astype(BF16)
    plane_rows = planes * rows
    lanes2 = spectrum.shape[1] // n_zg
    for i in range(3):
        for p in range(n_zg):
            a_send[i, p] = spectrum[i * plane_rows : (i + 1) * plane_rows, p * lanes2 : (p + 1) * lanes2]
    pl.semaphore_wait(barrier, n_xy + n_zg - 2)
    for i in range(3):
        exchange(a_send, a_recv, a_ss, a_rs, i, "zg")

    loads[2].wait()
    for i in range(3):
        arrived(a_recv, a_rs, i)
        operand = a_recv[i].reshape(n_zg * plane_rows, lanes2)
        b_send[i] = dot(tz[...], stacked(operand)).astype(BF16).reshape(b_send.shape[1:])
        exchange(b_send, b_recv, b_ss, b_rs, i, "xy")

    loads[3].wait()
    rows_x = n_xy * rows

    def forward_x(i, carry):
        arrived(b_recv, b_rs, i)
        operand = b_recv[i].reshape(rows_x, lanes2)
        spec[i] = dot(tx[...], stacked(operand)).astype(BF16)
        return carry

    lax.fori_loop(0, 3, forward_x, 0)

    loads[4].wait()
    loads[5].wait()
    block = lanes2 // 2
    length_x = spec.shape[1]
    step_rows = 32
    for i in range(3):

        def product(step, carry):
            at = pl.ds(pl.multiple_of(step * step_rows, step_rows), step_rows)
            real = jnp.zeros((step_rows, block), F32)
            imag = jnp.zeros((step_rows, block), F32)
            for j in range(3):
                c = pairing[i][j]
                factor = scale_ref[c, 0]
                g_re = green[0, c, at, :].astype(F32) * factor
                g_im = green[1, c, at, :].astype(F32) * factor
                s_re = spec[j, at, :block].astype(F32)
                s_im = spec[j, at, block:].astype(F32)
                real = real + g_re * s_re - g_im * s_im
                imag = imag + g_re * s_im + g_im * s_re
            prod[at, :block] = real.astype(BF16)
            prod[at, block:] = imag.astype(BF16)
            return carry

        lax.fori_loop(0, length_x // step_rows, product, 0)
        c_send[i] = dot(ux[...], stacked(prod[...])).astype(BF16).reshape(c_send.shape[1:])
        exchange(c_send, c_recv, c_ss, c_rs, i, "xy")

    loads[6].wait()
    for i in range(3):
        arrived(c_recv, c_rs, i)
        operand = c_recv[i].reshape(rows_x, lanes2)
        d_send[i] = dot(uz[...], stacked(operand)).astype(BF16).reshape(d_send.shape[1:])
        exchange(d_send, d_recv, d_ss, d_rs, i, "zg")

    loads[7].wait()
    for i in range(3):
        arrived(d_recv, d_rs, i)
        operand = jnp.concatenate([d_recv[i, p] for p in range(n_zg)], axis=1)
        back = dot(operand, uy[...])
        for r in range(2):
            part = back[:, r * width : (r + 1) * width].reshape(planes, rows, width)
            out_ref[r, i] = (field[r, i].astype(F32) - part * norm).astype(BF16)

    for send, ss in ((a_send, a_ss), (b_send, b_ss), (c_send, c_ss), (d_send, d_ss)):
        for i in range(3):
            arrived(send, ss, i)


def on_device(dipole_field, material, alpha_table, green_spectrum, green_scale):
    n_zg = lax.axis_size("zg")
    n_xy = lax.axis_size("xy")
    _, _, planes, rows, width = dipole_field.shape
    planes_z, rows_x = planes * n_zg, rows * n_xy
    tables = tables_of(width, planes_z, rows_x, n_zg, n_xy)
    norm = 1.0 / float(8 * width * planes_z * rows_x)
    green = green_spectrum.reshape(green_spectrum.shape[:2] + green_spectrum.shape[3:])
    block = 2 * width // n_zg
    plane_rows = planes * rows
    dma = lambda n: pltpu.SemaphoreType.DMA((n,))
    over_zg = pltpu.VMEM((3, n_zg, plane_rows, 2 * block), BF16)
    over_xy = pltpu.VMEM((3, n_xy, rows, 2 * block), BF16)
    anywhere = pl.BlockSpec(memory_space=pl.ANY)
    vmem = pl.BlockSpec(memory_space=pltpu.VMEM)
    smem = pl.BlockSpec(memory_space=pltpu.SMEM)
    return pl.pallas_call(
        functools.partial(kernel, n_zg, n_xy, norm),
        out_shape=jax.ShapeDtypeStruct(dipole_field.shape, BF16),
        in_specs=[anywhere, vmem, smem, anywhere, smem] + [anywhere] * 6,
        out_specs=vmem,
        scratch_shapes=[
            pltpu.VMEM(dipole_field.shape, BF16),
            pltpu.VMEM(green.shape, BF16),
        ]
        + [pltpu.VMEM(t.shape, BF16) for t in tables]
        + [
            pltpu.VMEM((3 * plane_rows, 2 * width), BF16),
            over_zg, over_zg, over_xy, over_xy,
            pltpu.VMEM((3, 2 * rows_x, 2 * block), BF16),
            pltpu.VMEM((2 * rows_x, 2 * block), BF16),
            over_xy, over_xy, over_zg, over_zg,
            dma(8),
        ]
        + [dma(3)] * 8,
        compiler_params=pltpu.CompilerParams(
            collective_id=0, has_side_effects=True, vmem_limit_bytes=56 * 1024 * 1024
        ),
        cost_estimate=pl.CostEstimate(flops=5_000_000_000, bytes_accessed=12_000_000, transcendentals=0),
    )(dipole_field, material, alpha_table, green, green_scale, *[jnp.asarray(t) for t in tables])


def solution(mesh):
    return jax.shard_map(
        on_device,
        mesh=mesh,
        in_specs=(
            P(None, None, "zg", "xy", None),
            P("zg", "xy", None),
            P(),
            P(None, None, "xy", None, "zg"),
            P(None, "xy"),
        ),
        out_specs=P(None, None, "zg", "xy", None),
        check_vma=False,
    )
```

profile of v0, /device:TPU:1, one launch (start us, length us, event | category | flops | bytes accessed | tf_op | source)
XLA Modules:
  0.0 53.1 jit_solution(12887869222516509531)
XLA Ops:
  0.0 1.3 %copy.14.scale_ref = f32[6,1]{1,0:T(8,128)} copy(f32[6,1]{0,1:T(1,128)} %param.15) | data formatting | bytes 48 | tf_op args[4]
  1.3 1.4 %copy.13.alpha_ref = f32[4,2,3,3]{3,2,1,0:T(4,128)} copy(f32[4,2,3,3]{0,1,3,2:T(2,128)} %param.13) | data formatting | bytes 576 | tf_op args[2]
  2.7 1.4 %copy.12.material_ref = s32[4,16,2]{2,1,0:T(8,128)} copy(s32[4,16,2]{1,2,0:T(2,128)} %param.12) | data formatting | bytes 1024 | tf_op args[1]
  4.1 47.3 %shard_map.109 = bf16[2,3,4,16,256]{4,3,2,1,0:T(8,128)(2,1)} custom-call(bf16[2,3,4,16,256]{4,3,2,1,0:T(8,128)(2,1)} %field_hbm.1, s32[4,16,2]{2,1,0:T(8,128)} %copy.12.material_ref, f32[4,2,3,3]{3,2,1,0:T(4,128)} %copy.13.alpha_ref, bf16[2,6,1024,128]{3,2,1,0:T(8,128)(2,1)} %bitcast.1, f32[6,1]{1,0:T(8,128)} %copy.14.scale_ref, ...), custom_call_target="tpu_custom_call" | custom-call | flops 5000000000 | bytes 12000000 | tf_op jit(solution)/shard_map/pallas_call | solution.py:244
  51.4 1.6 %copy.16 = bf16[2,3,4,16,256]{4,3,2,1,0:T(8,128)(2,1)} copy(bf16[2,3,4,16,256]{4,3,2,1,0:T(8,128)(2,1)} %shard_map.109) | data formatting | bytes 393216
where the time goes:
time: 53.4 us; the launch traced here: 53.1 us
  Pallas kernels  47.3 us (89%)
  local copies, waits for them, and re-layouts  5.75 us (11%)
    pallas_call x1, Pallas kernels, on_device(): pl.pallas_call(functools.partial(kernel, n_zg, n_xy, norm), out_shape=jax...  47.3 us
    unnamed x4, local copies, waits for them, and re-layouts  5.75 us

commit v1 on v0

--- a/solution.py
+++ b/solution.py
@@ -67,10 +67,10 @@
     n_zg, n_xy, norm,
     field_hbm, material_ref, alpha_ref, green_hbm, scale_ref,
     ty_hbm, tz_hbm, tx_hbm, ux_hbm, uz_hbm, uy_hbm,
-    out_ref,
+    out_hbm,
     field, green, ty, tz, tx, ux, uz, uy,
-    mom, a_send, a_recv, b_send, b_recv, spec, prod, c_send, c_recv, d_send, d_recv,
-    load_sem, a_ss, a_rs, b_ss, b_rs, c_ss, c_rs, d_ss, d_rs,
+    mom, a_send, a_recv, b_send, b_recv, spec, weighted, total, prod, c_send, c_recv, d_send, d_recv, out,
+    load_sem, store_sem, a_ss, a_rs, b_ss, b_rs, c_ss, c_rs, d_ss, d_rs,
 ):
     g = lax.axis_index("zg")
     q = lax.axis_index("xy")
@@ -83,7 +83,7 @@
             )
         )
     ]
-    for load in loads:
+    for load in loads[:3]:
         load.start()
 
     barrier = pltpu.get_barrier_semaphore()
@@ -104,16 +104,19 @@
     loads[0].wait()
     planes, rows, width = field.shape[2:]
     half = width // 2
+    diagonal = lax.broadcasted_iota(jnp.int32, (rows, rows), 0) == lax.broadcasted_iota(jnp.int32, (rows, rows), 1)
     for z in range(planes):
         for b in range(2):
             lanes = slice(b * half, (b + 1) * half)
-            which = jnp.broadcast_to(material_ref[z][:, b : b + 1], (rows, half))
-            masks = [which == m for m in range(3)]
+            across = jnp.broadcast_to(material_ref[z, b : b + 1, :].astype(F32), (rows, rows))
+            which = jnp.sum(jnp.where(diagonal, across, 0.0), axis=1, keepdims=True)
+            which = jnp.broadcast_to(which, (rows, half))
+            masks = [which == float(m) for m in range(3)]
 
             def tensor(r, i, j):
-                value = jnp.full((rows, half), alpha_ref[3, r, i, j], F32)
+                value = jnp.full((rows, half), alpha_ref[i, j, r, 3], F32)
                 for m in range(3):
-                    value = jnp.where(masks[m], alpha_ref[m, r, i, j], value)
+                    value = jnp.where(masks[m], alpha_ref[i, j, r, m], value)
                 return value
 
             values = [[field[r, j, z, :, lanes].astype(F32) for j in range(3)] for r in range(2)]
@@ -157,6 +160,8 @@
     pl.semaphore_wait(barrier, n_xy + n_zg - 2)
     for i in range(3):
         exchange(a_send, a_recv, a_ss, a_rs, i, "zg")
+    for load in loads[3:]:
+        load.start()
 
     loads[2].wait()
     for i in range(3):
@@ -165,44 +170,56 @@
         b_send[i] = dot(tz[...], stacked(operand)).astype(BF16).reshape(b_send.shape[1:])
         exchange(b_send, b_recv, b_ss, b_rs, i, "xy")
 
+    block = lanes2 // 2
+    length_x = prod.shape[0]
+    step_rows = 32
+    loads[4].wait()
+
+    def weigh(step, carry):
+        at = pl.ds(pl.multiple_of(step * step_rows, step_rows), step_rows)
+        for c in range(6):
+            for r in range(2):
+                weighted[r, c, at, :] = green[r, c, at, :].astype(F32) * scale_ref[0, c]
+        return carry
+
+    lax.fori_loop(0, length_x // step_rows, weigh, 0)
+
     loads[3].wait()
+    loads[5].wait()
     rows_x = n_xy * rows
 
-    def forward_x(i, carry):
-        arrived(b_recv, b_rs, i)
-        operand = b_recv[i].reshape(rows_x, lanes2)
-        spec[i] = dot(tx[...], stacked(operand)).astype(BF16)
-        return carry
-
-    lax.fori_loop(0, 3, forward_x, 0)
-
-    loads[4].wait()
-    loads[5].wait()
-    block = lanes2 // 2
-    length_x = spec.shape[1]
-    step_rows = 32
-    for i in range(3):
-
-        def product(step, carry):
+    def terms(spectrum, at, i, j):
+        c = pairing[i][j]
+        g_re, g_im = weighted[0, c, at, :], weighted[1, c, at, :]
+        s_re, s_im = spectrum[:, :block], spectrum[:, block:]
+        return g_re * s_re - g_im * s_im, g_re * s_im + g_im * s_re
+
+    for j in range(3):
+        arrived(b_recv, b_rs, j)
+        operand = b_recv[j].reshape(rows_x, lanes2)
+        spec[...] = dot(tx[...], stacked(operand)).astype(BF16)
+
+        def accumulate(step, carry, i, final):
             at = pl.ds(pl.multiple_of(step * step_rows, step_rows), step_rows)
-            real = jnp.zeros((step_rows, block), F32)
-            imag = jnp.zeros((step_rows, block), F32)
-            for j in range(3):
-                c = pairing[i][j]
-                factor = scale_ref[c, 0]
-                g_re = green[0, c, at, :].astype(F32) * factor
-                g_im = green[1, c, at, :].astype(F32) * factor
-                s_re = spec[j, at, :block].astype(F32)
-                s_im = spec[j, at, block:].astype(F32)
-                real = real + g_re * s_re - g_im * s_im
-                imag = imag + g_re * s_im + g_im * s_re
-            prod[at, :block] = real.astype(BF16)
-            prod[at, block:] = imag.astype(BF16)
+            spectrum = spec[at, :].astype(F32)
+            real, imag = terms(spectrum, at, i, j)
+            if j > 0:
+                real = real + total[i, at, :block]
+                imag = imag + total[i, at, block:]
+            if final:
+                prod[at, :block] = real.astype(BF16)
+                prod[at, block:] = imag.astype(BF16)
+            else:
+                total[i, at, :block] = real
+                total[i, at, block:] = imag
             return carry
 
-        lax.fori_loop(0, length_x // step_rows, product, 0)
-        c_send[i] = dot(ux[...], stacked(prod[...])).astype(BF16).reshape(c_send.shape[1:])
-        exchange(c_send, c_recv, c_ss, c_rs, i, "xy")
+        for i in range(3):
+            final = j == 2
+            lax.fori_loop(0, length_x // step_rows, functools.partial(accumulate, i=i, final=final), 0)
+            if final:
+                c_send[i] = dot(ux[...], stacked(prod[...])).astype(BF16).reshape(c_send.shape[1:])
+                exchange(c_send, c_recv, c_ss, c_rs, i, "xy")
 
     loads[6].wait()
     for i in range(3):
@@ -210,6 +227,9 @@
         operand = c_recv[i].reshape(rows_x, lanes2)
         d_send[i] = dot(uz[...], stacked(operand)).astype(BF16).reshape(d_send.shape[1:])
         exchange(d_send, d_recv, d_ss, d_rs, i, "zg")
+
+    def store_of(i):
+        return pltpu.make_async_copy(out.at[:, i], out_hbm.at[:, i], store_sem.at[i])
 
     loads[7].wait()
     for i in range(3):
@@ -218,11 +238,14 @@
         back = dot(operand, uy[...])
         for r in range(2):
             part = back[:, r * width : (r + 1) * width].reshape(planes, rows, width)
-            out_ref[r, i] = (field[r, i].astype(F32) - part * norm).astype(BF16)
+            out[r, i] = (field[r, i].astype(F32) - part * norm).astype(BF16)
+        store_of(i).start()
 
     for send, ss in ((a_send, a_ss), (b_send, b_ss), (c_send, c_ss), (d_send, d_ss)):
         for i in range(3):
             arrived(send, ss, i)
+    for i in range(3):
+        store_of(i).wait()
 
 
 def on_device(dipole_field, material, alpha_table, green_spectrum, green_scale):
@@ -233,6 +256,9 @@
     tables = tables_of(width, planes_z, rows_x, n_zg, n_xy)
     norm = 1.0 / float(8 * width * planes_z * rows_x)
     green = green_spectrum.reshape(green_spectrum.shape[:2] + green_spectrum.shape[3:])
+    material = material.transpose(0, 2, 1)
+    alpha_table = alpha_table.transpose(2, 3, 1, 0)
+    green_scale = green_scale.transpose(1, 0)
     block = 2 * width // n_zg
     plane_rows = planes * rows
     dma = lambda n: pltpu.SemaphoreType.DMA((n,))
@@ -245,7 +271,7 @@
         functools.partial(kernel, n_zg, n_xy, norm),
         out_shape=jax.ShapeDtypeStruct(dipole_field.shape, BF16),
         in_specs=[anywhere, vmem, smem, anywhere, smem] + [anywhere] * 6,
-        out_specs=vmem,
+        out_specs=anywhere,
         scratch_shapes=[
             pltpu.VMEM(dipole_field.shape, BF16),
             pltpu.VMEM(green.shape, BF16),
@@ -254,10 +280,13 @@
         + [
             pltpu.VMEM((3 * plane_rows, 2 * width), BF16),
             over_zg, over_zg, over_xy, over_xy,
-            pltpu.VMEM((3, 2 * rows_x, 2 * block), BF16),
+            pltpu.VMEM((2 * rows_x, 2 * block), BF16),
+            pltpu.VMEM(green.shape, F32),
+            pltpu.VMEM((3, 2 * rows_x, 2 * block), F32),
             pltpu.VMEM((2 * rows_x, 2 * block), BF16),
             over_xy, over_xy, over_zg, over_zg,
-            dma(8),
+            pltpu.VMEM(dipole_field.shape, BF16),
+            dma(8), dma(3),
         ]
         + [dma(3)] * 8,
         compiler_params=pltpu.CompilerParams(

time: 53.4 us -> 49 us (0.918)
  local copies, waits for them, and re-layouts: 5.75 us -> 1.62 us
    unnamed x4 -> x1, local copies, waits for them, and re-layouts: 5.75 us -> 1.62 us
where the time goes in v1:
time: 49 us; the launch traced here: 48.8 us
  Pallas kernels  47.2 us (96%)
  local copies, waits for them, and re-layouts  1.62 us (3%)
    pallas_call x1, Pallas kernels, on_device(): pl.pallas_call(functools.partial(kernel, n_zg, n_xy, norm), out_shape=jax...  47.2 us
    unnamed x1, local copies, waits for them, and re-layouts  1.62 us

profile of v1, /device:TPU:1, one launch (start us, length us, event | category | flops | bytes accessed | tf_op | source)
XLA Modules:
  0.0 48.8 jit_solution(5954060771905958908)
XLA Ops:
  0.0 47.2 %shard_map.109 = bf16[2,3,4,16,256]{4,3,2,1,0:T(8,128)(2,1)} custom-call(bf16[2,3,4,16,256]{4,3,2,1,0:T(8,128)(2,1)} %field_hbm.1, s32[4,2,16]{2,1,0:T(2,128)} %bitcast.6, f32[3,3,2,4]{3,2,1,0:T(2,128)} %bitcast.5, bf16[2,6,1024,128]{3,2,1,0:T(8,128)(2,1)} %bitcast.4, f32[1,6]{1,0:T(1,128)} %bitcast.7, bf16[512,1024]{1,0:T(8,128)(2,1)} %constant.12.clone.ty_hbm, ...), custom_call_target="tpu_custom_call" | custom-call | flops 5000000000 | bytes 12000000 | tf_op jit(solution)/shard_map/pallas_call | solution.py:270
  47.2 1.6 %copy.13 = bf16[2,3,4,16,256]{4,3,2,1,0:T(8,128)(2,1)} copy(bf16[2,3,4,16,256]{4,3,2,1,0:T(8,128)(2,1)} %shard_map.109) | data formatting | bytes 393216

commit v2 on v1

--- a/solution.py
+++ b/solution.py
@@ -59,6 +59,10 @@
     return jnp.concatenate([pair, times_i(pair)], axis=0)
 
 
+def far_first(d):
+    return 2 + d + (d // 2) * (1 - 2 * d)
+
+
 def dot(a, b):
     return jnp.dot(a, b, preferred_element_type=F32)
 
@@ -105,7 +109,7 @@
     planes, rows, width = field.shape[2:]
     half = width // 2
     diagonal = lax.broadcasted_iota(jnp.int32, (rows, rows), 0) == lax.broadcasted_iota(jnp.int32, (rows, rows), 1)
-    for z in range(planes):
+    def moments_of_plane(z, carry):
         for b in range(2):
             lanes = slice(b * half, (b + 1) * half)
             across = jnp.broadcast_to(material_ref[z, b : b + 1, :].astype(F32), (rows, rows))
@@ -127,15 +131,25 @@
                     t_re, t_im = tensor(0, i, j), tensor(1, i, j)
                     real = real + t_re * values[0][j] - t_im * values[1][j]
                     imag = imag + t_re * values[1][j] + t_im * values[0][j]
-                start = (i * planes + z) * rows
-                mom[start : start + rows, b * half : (b + 1) * half] = real.astype(BF16)
-                mom[start : start + rows, width + b * half : width + (b + 1) * half] = imag.astype(BF16)
+                mom[i, z, :, b * half : (b + 1) * half] = real.astype(BF16)
+                mom[i, z, :, width + b * half : width + (b + 1) * half] = imag.astype(BF16)
+        return carry
+
+    lax.fori_loop(0, planes, moments_of_plane, 0)
 
     def exchange(send, recv, ss, rs, index, axis):
         count, me = (n_zg, g) if axis == "zg" else (n_xy, q)
 
         def step_of(step, carry):
-            peer = lax.rem(me + step, count)
+            if axis == "xy" and count == 32:
+                x, y, z = lax.rem(q, 4), lax.rem(q // 4, 4), q // 16
+                k = step - 1
+                peer_x = lax.rem(x + far_first(lax.rem(k, 4)), 4)
+                peer_y = lax.rem(y + far_first(lax.rem(k // 4, 4)), 4)
+                peer_z = lax.rem(z + 1 - k // 16, 2)
+                peer = peer_z * 16 + peer_y * 4 + peer_x
+            else:
+                peer = lax.rem(me + step, count)
             target = (peer, q) if axis == "zg" else (g, peer)
             pltpu.make_async_remote_copy(
                 send.at[index, peer], recv.at[index, me], ss.at[index], rs.at[index],
@@ -151,7 +165,7 @@
         pltpu.make_async_copy(others, others, rs.at[index]).wait()
 
     loads[1].wait()
-    spectrum = dot(mom[...], ty[...]).astype(BF16)
+    spectrum = dot(mom[...].reshape(3 * planes * rows, 2 * width), ty[...]).astype(BF16)
     plane_rows = planes * rows
     lanes2 = spectrum.shape[1] // n_zg
     for i in range(3):
@@ -164,15 +178,19 @@
         load.start()
 
     loads[2].wait()
-    for i in range(3):
+
+    def forward_z(i, carry):
         arrived(a_recv, a_rs, i)
         operand = a_recv[i].reshape(n_zg * plane_rows, lanes2)
         b_send[i] = dot(tz[...], stacked(operand)).astype(BF16).reshape(b_send.shape[1:])
         exchange(b_send, b_recv, b_ss, b_rs, i, "xy")
+        return carry
+
+    lax.fori_loop(0, 3, forward_z, 0)
 
     block = lanes2 // 2
     length_x = prod.shape[0]
-    step_rows = 32
+    step_rows = 128
     loads[4].wait()
 
     def weigh(step, carry):
@@ -180,6 +198,8 @@
         for c in range(6):
             for r in range(2):
                 weighted[r, c, at, :] = green[r, c, at, :].astype(F32) * scale_ref[0, c]
+        for i in range(3):
+            total[i, at, :] = jnp.zeros((step_rows, lanes2), F32)
         return carry
 
     lax.fori_loop(0, length_x // step_rows, weigh, 0)
@@ -188,51 +208,63 @@
     loads[5].wait()
     rows_x = n_xy * rows
 
-    def terms(spectrum, at, i, j):
-        c = pairing[i][j]
+    def added(i, j, at):
+        c = jnp.where(i == j, i, i + j + 2)
+        spectrum = spec[at, :].astype(F32)
+        s_re, s_im = spectrum[:, :block], spectrum[:, block:]
         g_re, g_im = weighted[0, c, at, :], weighted[1, c, at, :]
-        s_re, s_im = spectrum[:, :block], spectrum[:, block:]
-        return g_re * s_re - g_im * s_im, g_re * s_im + g_im * s_re
-
-    for j in range(3):
+        real = total[i, at, :block] + g_re * s_re - g_im * s_im
+        imag = total[i, at, block:] + g_re * s_im + g_im * s_re
+        return real, imag
+
+    def forward_x(j, carry):
         arrived(b_recv, b_rs, j)
         operand = b_recv[j].reshape(rows_x, lanes2)
         spec[...] = dot(tx[...], stacked(operand)).astype(BF16)
 
-        def accumulate(step, carry, i, final):
+        def accumulate(step, carry):
             at = pl.ds(pl.multiple_of(step * step_rows, step_rows), step_rows)
-            spectrum = spec[at, :].astype(F32)
-            real, imag = terms(spectrum, at, i, j)
-            if j > 0:
-                real = real + total[i, at, :block]
-                imag = imag + total[i, at, block:]
-            if final:
-                prod[at, :block] = real.astype(BF16)
-                prod[at, block:] = imag.astype(BF16)
-            else:
+            for i in range(3):
+                real, imag = added(i, j, at)
                 total[i, at, :block] = real
                 total[i, at, block:] = imag
             return carry
 
-        for i in range(3):
-            final = j == 2
-            lax.fori_loop(0, length_x // step_rows, functools.partial(accumulate, i=i, final=final), 0)
-            if final:
-                c_send[i] = dot(ux[...], stacked(prod[...])).astype(BF16).reshape(c_send.shape[1:])
-                exchange(c_send, c_recv, c_ss, c_rs, i, "xy")
+        return lax.fori_loop(0, jnp.where(j < 2, length_x // step_rows, 0), accumulate, carry)
+
+    lax.fori_loop(0, 3, forward_x, 0)
+
+    def inverse_x(i, carry):
+        def finish(step, carry):
+            at = pl.ds(pl.multiple_of(step * step_rows, step_rows), step_rows)
+            real, imag = added(i, 2, at)
+            prod[at, :block] = real.astype(BF16)
+            prod[at, block:] = imag.astype(BF16)
+            return carry
+
+        lax.fori_loop(0, length_x // step_rows, finish, 0)
+        c_send[i] = dot(ux[...], stacked(prod[...])).astype(BF16).reshape(c_send.shape[1:])
+        exchange(c_send, c_recv, c_ss, c_rs, i, "xy")
+        return carry
+
+    lax.fori_loop(0, 3, inverse_x, 0)
 
     loads[6].wait()
-    for i in range(3):
+
+    def inverse_z(i, carry):
         arrived(c_recv, c_rs, i)
         operand = c_recv[i].reshape(rows_x, lanes2)
         d_send[i] = dot(uz[...], stacked(operand)).astype(BF16).reshape(d_send.shape[1:])
         exchange(d_send, d_recv, d_ss, d_rs, i, "zg")
+        return carry
+
+    lax.fori_loop(0, 3, inverse_z, 0)
 
     def store_of(i):
         return pltpu.make_async_copy(out.at[:, i], out_hbm.at[:, i], store_sem.at[i])
 
     loads[7].wait()
-    for i in range(3):
+    def inverse_y(i, carry):
         arrived(d_recv, d_rs, i)
         operand = jnp.concatenate([d_recv[i, p] for p in range(n_zg)], axis=1)
         back = dot(operand, uy[...])
@@ -240,6 +272,9 @@
             part = back[:, r * width : (r + 1) * width].reshape(planes, rows, width)
             out[r, i] = (field[r, i].astype(F32) - part * norm).astype(BF16)
         store_of(i).start()
+        return carry
+
+    lax.fori_loop(0, 3, inverse_y, 0)
 
     for send, ss in ((a_send, a_ss), (b_send, b_ss), (c_send, c_ss), (d_send, d_ss)):
         for i in range(3):
@@ -278,7 +313,7 @@
         ]
         + [pltpu.VMEM(t.shape, BF16) for t in tables]
         + [
-            pltpu.VMEM((3 * plane_rows, 2 * width), BF16),
+            pltpu.VMEM((3, planes, rows, 2 * width), BF16),
             over_zg, over_zg, over_xy, over_xy,
             pltpu.VMEM((2 * rows_x, 2 * block), BF16),
             pltpu.VMEM(green.shape, F32),

time: 49 us -> 46.5 us (0.949)
  Pallas kernels: 47.2 us -> 44.7 us
    pallas_call x1, Pallas kernels: 47.2 us -> 44.7 us  [on_device(): pl.pallas_call(functools.partial(kernel, n_zg, n_xy, norm), out_shape=jax...]
where the time goes in v2:
time: 46.5 us; the launch traced here: 46.3 us
  Pallas kernels  44.7 us (96%)
  local copies, waits for them, and re-layouts  1.62 us (3%)
    pallas_call x1, Pallas kernels, on_device(): pl.pallas_call(functools.partial(kernel, n_zg, n_xy, norm), out_shape=jax...  44.7 us
    unnamed x1, local copies, waits for them, and re-layouts  1.62 us

profile of v2, /device:TPU:1, one launch (start us, length us, event | category | flops | bytes accessed | tf_op | source)
XLA Modules:
  0.0 46.3 jit_solution(9573976618930471334)
XLA Ops:
  0.0 44.7 %shard_map.109 = bf16[2,3,4,16,256]{4,3,2,1,0:T(8,128)(2,1)} custom-call(bf16[2,3,4,16,256]{4,3,2,1,0:T(8,128)(2,1)} %field_hbm.1, s32[4,2,16]{2,1,0:T(2,128)} %bitcast.6, f32[3,3,2,4]{3,2,1,0:T(2,128)} %bitcast.5, bf16[2,6,1024,128]{3,2,1,0:T(8,128)(2,1)} %bitcast.4, f32[1,6]{1,0:T(1,128)} %bitcast.7, bf16[512,1024]{1,0:T(8,128)(2,1)} %constant.12.clone.ty_hbm, ...), custom_call_target="tpu_custom_call" | custom-call | flops 5000000000 | bytes 12000000 | tf_op jit(solution)/shard_map/pallas_call | solution.py:305
  44.7 1.6 %copy.13 = bf16[2,3,4,16,256]{4,3,2,1,0:T(8,128)(2,1)} copy(bf16[2,3,4,16,256]{4,3,2,1,0:T(8,128)(2,1)} %shard_map.109) | data formatting | bytes 393216

commit v3 on v2

--- a/solution.py
+++ b/solution.py
@@ -71,10 +71,10 @@
     n_zg, n_xy, norm,
     field_hbm, material_ref, alpha_ref, green_hbm, scale_ref,
     ty_hbm, tz_hbm, tx_hbm, ux_hbm, uz_hbm, uy_hbm,
-    out_hbm,
+    out,
     field, green, ty, tz, tx, ux, uz, uy,
-    mom, a_send, a_recv, b_send, b_recv, spec, weighted, total, prod, c_send, c_recv, d_send, d_recv, out,
-    load_sem, store_sem, a_ss, a_rs, b_ss, b_rs, c_ss, c_rs, d_ss, d_rs,
+    mom, a_send, a_recv, b_send, b_recv, spec, weighted, total, prod, c_send, c_recv, d_send, d_recv,
+    load_sem, a_ss, a_rs, b_ss, b_rs, c_ss, c_rs, d_ss, d_rs,
 ):
     g = lax.axis_index("zg")
     q = lax.axis_index("xy")
@@ -260,9 +260,6 @@
 
     lax.fori_loop(0, 3, inverse_z, 0)
 
-    def store_of(i):
-        return pltpu.make_async_copy(out.at[:, i], out_hbm.at[:, i], store_sem.at[i])
-
     loads[7].wait()
     def inverse_y(i, carry):
         arrived(d_recv, d_rs, i)
@@ -271,7 +268,6 @@
         for r in range(2):
             part = back[:, r * width : (r + 1) * width].reshape(planes, rows, width)
             out[r, i] = (field[r, i].astype(F32) - part * norm).astype(BF16)
-        store_of(i).start()
         return carry
 
     lax.fori_loop(0, 3, inverse_y, 0)
@@ -279,8 +275,12 @@
     for send, ss in ((a_send, a_ss), (b_send, b_ss), (c_send, c_ss), (d_send, d_ss)):
         for i in range(3):
             arrived(send, ss, i)
-    for i in range(3):
-        store_of(i).wait()
+
+
+def hand_out(held_ref, out_hbm, sem):
+    store = pltpu.make_async_copy(held_ref, out_hbm, sem)
+    store.start()
+    store.wait()
 
 
 def on_device(dipole_field, material, alpha_table, green_spectrum, green_scale):
@@ -302,11 +302,13 @@
     anywhere = pl.BlockSpec(memory_space=pl.ANY)
     vmem = pl.BlockSpec(memory_space=pltpu.VMEM)
     smem = pl.BlockSpec(memory_space=pltpu.SMEM)
-    return pl.pallas_call(
+    operands = [dipole_field, material, alpha_table, green, green_scale, *[jnp.asarray(t) for t in tables]]
+    operands = [pltpu.with_memory_space_constraint(x, pltpu.HBM) for x in operands]
+    held = pl.pallas_call(
         functools.partial(kernel, n_zg, n_xy, norm),
         out_shape=jax.ShapeDtypeStruct(dipole_field.shape, BF16),
         in_specs=[anywhere, vmem, smem, anywhere, smem] + [anywhere] * 6,
-        out_specs=anywhere,
+        out_specs=vmem,
         scratch_shapes=[
             pltpu.VMEM(dipole_field.shape, BF16),
             pltpu.VMEM(green.shape, BF16),
@@ -320,15 +322,22 @@
             pltpu.VMEM((3, 2 * rows_x, 2 * block), F32),
             pltpu.VMEM((2 * rows_x, 2 * block), BF16),
             over_xy, over_xy, over_zg, over_zg,
-            pltpu.VMEM(dipole_field.shape, BF16),
-            dma(8), dma(3),
+            dma(8),
         ]
         + [dma(3)] * 8,
         compiler_params=pltpu.CompilerParams(
-            collective_id=0, has_side_effects=True, vmem_limit_bytes=56 * 1024 * 1024
+            collective_id=0, has_side_effects=True, vmem_limit_bytes=48 * 1024 * 1024
         ),
         cost_estimate=pl.CostEstimate(flops=5_000_000_000, bytes_accessed=12_000_000, transcendentals=0),
-    )(dipole_field, material, alpha_table, green, green_scale, *[jnp.asarray(t) for t in tables])
+    )(*operands)
+    return pl.pallas_call(
+        hand_out,
+        out_shape=jax.ShapeDtypeStruct(dipole_field.shape, BF16),
+        in_specs=[vmem],
+        out_specs=anywhere,
+        scratch_shapes=[pltpu.SemaphoreType.DMA],
+        compiler_params=pltpu.CompilerParams(vmem_limit_bytes=4 * 1024 * 1024),
+    )(held)
 
 
 def solution(mesh):

time: 46.5 us -> 45 us (0.968)
  local copies, waits for them, and re-layouts: 1.62 us -> 0 us
    unnamed x1 -> x0, local copies, waits for them, and re-layouts: 1.62 us -> none
    pallas_call x0 -> x1, Pallas kernels: none -> 0.69 us  [on_device(): pl.pallas_call(hand_out, out_shape=jax.ShapeDtypeStruct(dipole_field.shap...]
    pallas_call x1, Pallas kernels: 44.7 us -> 44.1 us  [on_device(): pl.pallas_call(functools.partial(kernel, n_zg, n_xy, norm), out_shape=jax...]
where the time goes in v3:
time: 45 us; the launch traced here: 44.8 us
  Pallas kernels  44.8 us (100%)
    pallas_call x1, Pallas kernels, on_device(): pl.pallas_call(functools.partial(kernel, n_zg, n_xy, norm), out_shape=jax...  44.1 us

profile of v3, /device:TPU:1, one launch (start us, length us, event | category | flops | bytes accessed | tf_op | source)
XLA Modules:
  0.0 44.8 jit_solution(3978939631843420945)
XLA Ops:
  0.0 44.1 %shard_map.109.held_ref = bf16[2,3,4,16,256]{4,3,2,1,0:T(8,128)(2,1)S(1)} custom-call(bf16[2,3,4,16,256]{4,3,2,1,0:T(8,128)(2,1)} %field_hbm.1, s32[4,2,16]{2,1,0:T(2,128)} %bitcast.6, f32[3,3,2,4]{3,2,1,0:T(2,128)} %bitcast.5, bf16[2,6,1024,128]{3,2,1,0:T(8,128)(2,1)} %bitcast.4, f32[1,6]{1,0:T(1,128)} %bitcast.7, bf16[512,1024]{1,0:T(8,128)(2,1)} %constant.12.clone.ty_hbm, ...), custom_call_target="tpu_custom_call" | custom-call | flops 5000000000 | bytes 12000000 | tf_op jit(solution)/shard_map/pallas_call | solution.py:307
  44.1 0.7 %shard_map.110 = bf16[2,3,4,16,256]{4,3,2,1,0:T(8,128)(2,1)} custom-call(bf16[2,3,4,16,256]{4,3,2,1,0:T(8,128)(2,1)S(1)} %shard_map.109.held_ref), custom_call_target="tpu_custom_call" | custom-call | tf_op jit(solution)/shard_map/pallas_call | solution.py:333

commit v4 on v3

--- a/solution.py
+++ b/solution.py
@@ -30,17 +30,20 @@
     block_y = length_y // n_zg
     local_x = rows_x // n_xy
     eye = np.eye(local_x, dtype=np.float32)
+    eye = np.concatenate([eye[0::2], eye[1::2]])
     c, s = dft_table(rows_y, length_y, length_y, -1.0)
     full = np.block([[c, s], [-s, c]]).reshape(2 * rows_y, 2, n_zg, block_y)
     forward_y = full.transpose(0, 2, 1, 3).reshape(2 * rows_y, 2 * length_y)
     c, s = dft_table(planes_z, length_z, length_z, -1.0)
     forward_z = np.concatenate([np.kron(c.T, eye), np.kron(s.T, eye)], axis=1)
     c, s = dft_table(rows_x, length_x, length_x, -1.0)
-    forward_x = np.concatenate([c.T, s.T], axis=1)
+    c, s = c[:, :rows_x], s[:, :rows_x]
+    forward_x = np.stack([np.concatenate([c[p::2].T, s[p::2].T], axis=1) for p in range(2)])
     c, s = dft_table(length_x, rows_x, length_x, 1.0)
-    inverse_x = np.concatenate([c.T, s.T], axis=1)
+    c, s = c[:rows_x], s[:rows_x]
+    inverse_x = np.stack([np.concatenate([c[:, p::2].T, s[:, p::2].T], axis=1) for p in range(2)])
     c, s = dft_table(length_z, planes_z, length_z, 1.0)
-    inverse_z = np.concatenate([np.kron(c.T, eye), np.kron(s.T, eye)], axis=1)
+    inverse_z = np.concatenate([np.kron(c.T, eye.T), np.kron(s.T, eye.T)], axis=1)
     c, s = dft_table(length_y, rows_y, length_y, 1.0)
     full = np.block([[c, s], [-s, c]]).reshape(2, n_zg, block_y, 2 * rows_y)
     inverse_y = full.transpose(1, 0, 2, 3).reshape(2 * length_y, 2 * rows_y)
@@ -189,8 +192,10 @@
     lax.fori_loop(0, 3, forward_z, 0)
 
     block = lanes2 // 2
-    length_x = prod.shape[0]
+    half_x = prod.shape[1]
+    length_x = 2 * half_x
     step_rows = 128
+    finish_rows = 64
     loads[4].wait()
 
     def weigh(step, carry):
@@ -219,8 +224,13 @@
 
     def forward_x(j, carry):
         arrived(b_recv, b_rs, j)
-        operand = b_recv[j].reshape(rows_x, lanes2)
-        spec[...] = dot(tx[...], stacked(operand)).astype(BF16)
+        wide = b_recv[j].astype(F32)
+        even = wide[:, : rows // 2].reshape(half_x // 2, lanes2).astype(BF16)
+        odd = wide[:, rows // 2 :].reshape(half_x // 2, lanes2).astype(BF16)
+        even = dot(tx[0], stacked(even))
+        odd = dot(tx[1], stacked(odd))
+        spec[:half_x] = (even + odd).astype(BF16)
+        spec[half_x:] = (even - odd).astype(BF16)
 
         def accumulate(step, carry):
             at = pl.ds(pl.multiple_of(step * step_rows, step_rows), step_rows)
@@ -236,14 +246,18 @@
 
     def inverse_x(i, carry):
         def finish(step, carry):
-            at = pl.ds(pl.multiple_of(step * step_rows, step_rows), step_rows)
-            real, imag = added(i, 2, at)
-            prod[at, :block] = real.astype(BF16)
-            prod[at, block:] = imag.astype(BF16)
+            start = step * finish_rows
+            at = pl.ds(pl.multiple_of(start, finish_rows), finish_rows)
+            low = added(i, 2, at)
+            high = added(i, 2, pl.ds(pl.multiple_of(start + half_x, finish_rows), finish_rows))
+            for r in range(2):
+                prod[0, at, r * block : (r + 1) * block] = (low[r] + high[r]).astype(BF16)
+                prod[1, at, r * block : (r + 1) * block] = (low[r] - high[r]).astype(BF16)
             return carry
 
-        lax.fori_loop(0, length_x // step_rows, finish, 0)
-        c_send[i] = dot(ux[...], stacked(prod[...])).astype(BF16).reshape(c_send.shape[1:])
+        lax.fori_loop(0, half_x // finish_rows, finish, 0)
+        parts = [dot(ux[p], stacked(prod[p])).reshape(n_xy, rows // 2, lanes2) for p in range(2)]
+        c_send[i] = jnp.concatenate(parts, axis=1).astype(BF16)
         exchange(c_send, c_recv, c_ss, c_rs, i, "xy")
         return carry
 
@@ -320,7 +334,7 @@
             pltpu.VMEM((2 * rows_x, 2 * block), BF16),
             pltpu.VMEM(green.shape, F32),
             pltpu.VMEM((3, 2 * rows_x, 2 * block), F32),
-            pltpu.VMEM((2 * rows_x, 2 * block), BF16),
+            pltpu.VMEM((2, rows_x, 2 * block), BF16),
             over_xy, over_xy, over_zg, over_zg,
             dma(8),
         ]

time: 45 us -> 44.2 us (0.982)
  Pallas kernels: 44.8 us -> 44 us
    pallas_call x1, Pallas kernels: 44.1 us -> 43.3 us  [on_device(): pl.pallas_call(functools.partial(kernel, n_zg, n_xy, norm), out_shape=jax...]
where the time goes in v4:
time: 44.2 us; the launch traced here: 44 us
  Pallas kernels  44 us (100%)
    pallas_call x1, Pallas kernels, on_device(): pl.pallas_call(functools.partial(kernel, n_zg, n_xy, norm), out_shape=jax...  43.3 us

profile of v4, /device:TPU:1, one launch (start us, length us, event | category | flops | bytes accessed | tf_op | source)
XLA Modules:
  0.0 44.0 jit_solution(451437406266803678)
XLA Ops:
  0.0 43.3 %shard_map.109.held_ref = bf16[2,3,4,16,256]{4,3,2,1,0:T(8,128)(2,1)S(1)} custom-call(bf16[2,3,4,16,256]{4,3,2,1,0:T(8,128)(2,1)} %field_hbm.1, s32[4,2,16]{2,1,0:T(2,128)} %bitcast.6, f32[3,3,2,4]{3,2,1,0:T(2,128)} %bitcast.5, bf16[2,6,1024,128]{3,2,1,0:T(8,128)(2,1)} %bitcast.4, f32[1,6]{1,0:T(1,128)} %bitcast.7, bf16[512,1024]{1,0:T(8,128)(2,1)} %constant.12.clone.ty_hbm, ...), custom_call_target="tpu_custom_call" | custom-call | flops 5000000000 | bytes 12000000 | tf_op jit(solution)/shard_map/pallas_call | solution.py:321
  43.3 0.7 %shard_map.110 = bf16[2,3,4,16,256]{4,3,2,1,0:T(8,128)(2,1)} custom-call(bf16[2,3,4,16,256]{4,3,2,1,0:T(8,128)(2,1)S(1)} %shard_map.109.held_ref), custom_call_target="tpu_custom_call" | custom-call | tf_op jit(solution)/shard_map/pallas_call | solution.py:347

commit v5 on v4

--- a/solution.py
+++ b/solution.py
@@ -77,7 +77,7 @@
     out,
     field, green, ty, tz, tx, ux, uz, uy,
     mom, a_send, a_recv, b_send, b_recv, spec, weighted, total, prod, c_send, c_recv, d_send, d_recv,
-    load_sem, a_ss, a_rs, b_ss, b_rs, c_ss, c_rs, d_ss, d_rs,
+    load_sem, a_ss, a_rs, b_ss, b_rs, c_ss, c_rs, d_ss, d_rs, row_sem, plane_sem,
 ):
     g = lax.axis_index("zg")
     q = lax.axis_index("xy")
@@ -95,18 +95,13 @@
 
     barrier = pltpu.get_barrier_semaphore()
 
-    def greet_xy(step, carry):
-        peer = lax.rem(q + step, n_xy)
-        pl.semaphore_signal(barrier, inc=1, device_id=(g, peer), device_id_type=MESH)
-        return carry
-
-    def greet_zg(step, carry):
-        peer = lax.rem(g + step, n_zg)
-        pl.semaphore_signal(barrier, inc=1, device_id=(peer, q), device_id_type=MESH)
-        return carry
-
-    lax.fori_loop(1, n_xy, greet_xy, 0)
-    lax.fori_loop(1, n_zg, greet_zg, 0)
+    x, y, zl = lax.rem(q, 4), lax.rem(q // 4, 4), q // 16
+    peers_x = [(g, q - x + lax.rem(x + step, 4)) for step in (2, 1, 3)]
+    peers_y = [(g, q + 4 * (lax.rem(y + step, 4) - y)) for step in (2, 1, 3)]
+    peer_zl = (g, lax.rem(q + 16, 32))
+    peers_zg = [(lax.rem(g + step, n_zg), q) for step in (2, 1, 3)]
+    for peer in peers_zg + peers_x + peers_y + [peer_zl]:
+        pl.semaphore_signal(barrier, inc=1, device_id=peer, device_id_type=MESH)
 
     loads[0].wait()
     planes, rows, width = field.shape[2:]
@@ -174,18 +169,28 @@
     for i in range(3):
         for p in range(n_zg):
             a_send[i, p] = spectrum[i * plane_rows : (i + 1) * plane_rows, p * lanes2 : (p + 1) * lanes2]
-    pl.semaphore_wait(barrier, n_xy + n_zg - 2)
+    pl.semaphore_wait(barrier, 10)
+    for peer in peers_y:
+        pl.semaphore_signal(row_sem, inc=1, device_id=peer, device_id_type=MESH)
     for i in range(3):
         exchange(a_send, a_recv, a_ss, a_rs, i, "zg")
     for load in loads[3:]:
         load.start()
 
+    pl.semaphore_wait(row_sem, 3)
+    pl.semaphore_signal(plane_sem, inc=1, device_id=peer_zl, device_id_type=MESH)
+
     loads[2].wait()
 
     def forward_z(i, carry):
         arrived(a_recv, a_rs, i)
         operand = a_recv[i].reshape(n_zg * plane_rows, lanes2)
         b_send[i] = dot(tz[...], stacked(operand)).astype(BF16).reshape(b_send.shape[1:])
+
+        @pl.when(i == 0)
+        def _():
+            pl.semaphore_wait(plane_sem, 1)
+
         exchange(b_send, b_recv, b_ss, b_rs, i, "xy")
         return carry
 
@@ -338,7 +343,8 @@
             over_xy, over_xy, over_zg, over_zg,
             dma(8),
         ]
-        + [dma(3)] * 8,
+        + [dma(3)] * 8
+        + [pltpu.SemaphoreType.REGULAR] * 2,
         compiler_params=pltpu.CompilerParams(
             collective_id=0, has_side_effects=True, vmem_limit_bytes=48 * 1024 * 1024
         ),

time: 44.2 us -> 44.2 us (level)
  no operation moved by 1% of the time
where the time goes in v5:
time: 44.2 us; the launch traced here: 44 us
  Pallas kernels  44 us (100%)
    pallas_call x1, Pallas kernels, on_device(): pl.pallas_call(functools.partial(kernel, n_zg, n_xy, norm), out_shape=jax...  43.4 us

profile of v5, /device:TPU:1, one launch (start us, length us, event | category | flops | bytes accessed | tf_op | source)
XLA Modules:
  0.0 44.0 jit_solution(6431919450749504738)
XLA Ops:
  0.0 43.4 %shard_map.109.held_ref = bf16[2,3,4,16,256]{4,3,2,1,0:T(8,128)(2,1)S(1)} custom-call(bf16[2,3,4,16,256]{4,3,2,1,0:T(8,128)(2,1)} %field_hbm.1, s32[4,2,16]{2,1,0:T(2,128)} %bitcast.6, f32[3,3,2,4]{3,2,1,0:T(2,128)} %bitcast.5, bf16[2,6,1024,128]{3,2,1,0:T(8,128)(2,1)} %bitcast.4, f32[1,6]{1,0:T(1,128)} %bitcast.7, bf16[512,1024]{1,0:T(8,128)(2,1)} %constant.12.clone.ty_hbm, ...), custom_call_target="tpu_custom_call" | custom-call | flops 5000000000 | bytes 12000000 | tf_op jit(solution)/shard_map/pallas_call | solution.py:326
  43.4 0.7 %shard_map.110 = bf16[2,3,4,16,256]{4,3,2,1,0:T(8,128)(2,1)} custom-call(bf16[2,3,4,16,256]{4,3,2,1,0:T(8,128)(2,1)S(1)} %shard_map.109.held_ref), custom_call_target="tpu_custom_call" | custom-call | tf_op jit(solution)/shard_map/pallas_call | solution.py:353

commit v6 on v5

--- a/solution.py
+++ b/solution.py
@@ -14,7 +14,10 @@
 F32 = jnp.float32
 BF16 = jnp.bfloat16
 
-pairing = ((0, 3, 4), (3, 1, 5), (4, 5, 2))
+xy_steps = sorted(
+    [(zl, y, x) for zl in range(2) for y in range(4) for x in range(4) if (zl, y, x) != (0, 0, 0)],
+    key=lambda s: (-s[0], -min(s[1], 4 - s[1]) - min(s[2], 4 - s[2])),
+)
 
 
 def dft_table(count_in, count_out, length, direction):
@@ -158,22 +161,42 @@
         lax.fori_loop(1, count, step_of, 0)
         recv[index, me] = send[index, me]
 
+    at_x = [lax.rem(x + step, 4) for step in range(4)]
+    at_y = [lax.rem(y + step, 4) * 4 for step in range(4)]
+    at_zl = [zl * 16, lax.rem(zl + 1, 2) * 16]
+
+    def exchange_xy(send, recv, ss, rs, index):
+        for s_zl, s_y, s_x in xy_steps:
+            peer = at_zl[s_zl] + at_y[s_y] + at_x[s_x]
+            pltpu.make_async_remote_copy(
+                send.at[index, peer], recv.at[index, q], ss.at[index], rs.at[index],
+                device_id=(g, peer), device_id_type=MESH,
+            ).start()
+        recv[index, q] = send[index, q]
+
     def arrived(recv, rs, index):
         others = recv.at[index, pl.ds(0, recv.shape[1] - 1)]
         pltpu.make_async_copy(others, others, rs.at[index]).wait()
 
     loads[1].wait()
-    spectrum = dot(mom[...].reshape(3 * planes * rows, 2 * width), ty[...]).astype(BF16)
     plane_rows = planes * rows
-    lanes2 = spectrum.shape[1] // n_zg
-    for i in range(3):
+    lanes2 = ty.shape[1] // n_zg
+
+    def forward_y(i, carry):
+        spectrum = dot(mom[i].reshape(plane_rows, 2 * width), ty[...]).astype(BF16)
         for p in range(n_zg):
-            a_send[i, p] = spectrum[i * plane_rows : (i + 1) * plane_rows, p * lanes2 : (p + 1) * lanes2]
-    pl.semaphore_wait(barrier, 10)
-    for peer in peers_y:
-        pl.semaphore_signal(row_sem, inc=1, device_id=peer, device_id_type=MESH)
-    for i in range(3):
+            a_send[i, p] = spectrum[:, p * lanes2 : (p + 1) * lanes2]
+
+        @pl.when(i == 0)
+        def _():
+            pl.semaphore_wait(barrier, 10)
+            for peer in peers_y:
+                pl.semaphore_signal(row_sem, inc=1, device_id=peer, device_id_type=MESH)
+
         exchange(a_send, a_recv, a_ss, a_rs, i, "zg")
+        return carry
+
+    lax.fori_loop(0, 3, forward_y, 0)
     for load in loads[3:]:
         load.start()
 
@@ -191,7 +214,7 @@
         def _():
             pl.semaphore_wait(plane_sem, 1)
 
-        exchange(b_send, b_recv, b_ss, b_rs, i, "xy")
+        exchange_xy(b_send, b_recv, b_ss, b_rs, i)
         return carry
 
     lax.fori_loop(0, 3, forward_z, 0)
@@ -263,7 +286,7 @@
         lax.fori_loop(0, half_x // finish_rows, finish, 0)
         parts = [dot(ux[p], stacked(prod[p])).reshape(n_xy, rows // 2, lanes2) for p in range(2)]
         c_send[i] = jnp.concatenate(parts, axis=1).astype(BF16)
-        exchange(c_send, c_recv, c_ss, c_rs, i, "xy")
+        exchange_xy(c_send, c_recv, c_ss, c_rs, i)
         return carry
 
     lax.fori_loop(0, 3, inverse_x, 0)

time: 44.2 us -> 42.8 us (0.968)
  Pallas kernels: 44 us -> 42.7 us
    pallas_call x1, Pallas kernels: 43.4 us -> 42 us  [on_device(): pl.pallas_call(functools.partial(kernel, n_zg, n_xy, norm), out_shape=jax...]
where the time goes in v6:
time: 42.8 us; the launch traced here: 42.7 us
  Pallas kernels  42.7 us (100%)
    pallas_call x1, Pallas kernels, on_device(): pl.pallas_call(functools.partial(kernel, n_zg, n_xy, norm), out_shape=jax...  42 us

profile of v6, /device:TPU:1, one launch (start us, length us, event | category | flops | bytes accessed | tf_op | source)
XLA Modules:
  0.0 42.7 jit_solution(2929676225357450487)
XLA Ops:
  0.0 42.0 %shard_map.109.held_ref = bf16[2,3,4,16,256]{4,3,2,1,0:T(8,128)(2,1)S(1)} custom-call(bf16[2,3,4,16,256]{4,3,2,1,0:T(8,128)(2,1)} %field_hbm.1, s32[4,2,16]{2,1,0:T(2,128)} %bitcast.6, f32[3,3,2,4]{3,2,1,0:T(2,128)} %bitcast.5, bf16[2,6,1024,128]{3,2,1,0:T(8,128)(2,1)} %bitcast.4, f32[1,6]{1,0:T(1,128)} %bitcast.7, bf16[512,1024]{1,0:T(8,128)(2,1)} %constant.12.clone.ty_hbm, ...), custom_call_target="tpu_custom_call" | custom-call | flops 5000000000 | bytes 12000000 | tf_op jit(solution)/shard_map/pallas_call | solution.py:349
  42.0 0.7 %shard_map.110 = bf16[2,3,4,16,256]{4,3,2,1,0:T(8,128)(2,1)} custom-call(bf16[2,3,4,16,256]{4,3,2,1,0:T(8,128)(2,1)S(1)} %shard_map.109.held_ref), custom_call_target="tpu_custom_call" | custom-call | tf_op jit(solution)/shard_map/pallas_call | solution.py:376

commit v7 on v6

--- a/solution.py
+++ b/solution.py
@@ -158,7 +158,8 @@
             ).start()
             return carry
 
-        lax.fori_loop(1, count, step_of, 0)
+        for step in range(1, count):
+            step_of(step, 0)
         recv[index, me] = send[index, me]
 
     at_x = [lax.rem(x + step, 4) for step in range(4)]

time: 42.8 us -> 43.3 us (1.012)
    pallas_call x1, Pallas kernels: 42 us -> 42.5 us  [on_device(): pl.pallas_call(functools.partial(kernel, n_zg, n_xy, norm), out_shape=jax...]
where the time goes in v7:
time: 43.3 us; the launch traced here: 43.2 us
  Pallas kernels  43.1 us (100%)
    pallas_call x1, Pallas kernels, on_device(): pl.pallas_call(functools.partial(kernel, n_zg, n_xy, norm), out_shape=jax...  42.5 us

profile of v7, /device:TPU:1, one launch (start us, length us, event | category | flops | bytes accessed | tf_op | source)
XLA Modules:
  0.0 43.2 jit_solution(17546601587524853681)
XLA Ops:
  0.0 42.5 %shard_map.109.held_ref = bf16[2,3,4,16,256]{4,3,2,1,0:T(8,128)(2,1)S(1)} custom-call(bf16[2,3,4,16,256]{4,3,2,1,0:T(8,128)(2,1)} %field_hbm.1, s32[4,2,16]{2,1,0:T(2,128)} %bitcast.6, f32[3,3,2,4]{3,2,1,0:T(2,128)} %bitcast.5, bf16[2,6,1024,128]{3,2,1,0:T(8,128)(2,1)} %bitcast.4, f32[1,6]{1,0:T(1,128)} %bitcast.7, bf16[512,1024]{1,0:T(8,128)(2,1)} %constant.12.clone.ty_hbm, ...), custom_call_target="tpu_custom_call" | custom-call | flops 5000000000 | bytes 12000000 | tf_op jit(solution)/shard_map/pallas_call | solution.py:350
  42.5 0.7 %shard_map.110 = bf16[2,3,4,16,256]{4,3,2,1,0:T(8,128)(2,1)} custom-call(bf16[2,3,4,16,256]{4,3,2,1,0:T(8,128)(2,1)S(1)} %shard_map.109.held_ref), custom_call_target="tpu_custom_call" | custom-call | tf_op jit(solution)/shard_map/pallas_call | solution.py:377
